TPU v7x, 32 devices: a whole 2x2x4 slice. The times are simulated.
32 devices in a mesh: sky: 16 (over z, y, core), epoch: 2 (over x).
Axes of the slice: x: 2, y: 2, z: 4, core: 2. Of those that a mesh axis runs over, the one named last changes fastest.
Arguments:
- visits: float32 [2, 2048, 1024], P('epoch', 'sky'), may hold values from -6 to 6
- template: float32 [2048, 1024], P(('sky', 'epoch')), may hold values from -6 to 6
- basis_taps: float32 [2, 27, 17], replicated, may hold values from -1.5 to 1.5
- coeffs: float32 [2, 16, 27, 3], P('epoch', 'sky'), may hold values from -1.2 to 1.2
- psf_taps: float32 [2, 9], P('epoch'), may hold values from -2 to 2
- inv_var: float32 [2, 2048, 1024], P('epoch', 'sky'), may hold values from 0.3 to 3
- shifts: int32 [16, 24, 2, 2], P('sky'), may hold values from -16 to 16
- vel_count: int32 [16], P('sky'), may hold values from 1 to 24, 192 in all
Outputs:
- best_map: float32 [2048, 1024], P(('sky', 'epoch'))
Inputs may be any that keep to these rules, and one draw needn't show every extreme that they name: `shifts`: a velocity's shift of one epoch, row first, in whole pixels. Velocities 0 to vel_count - 1 of a tile are searched; some tile searches all 24.
All inputs are finite; a program needn't handle non-finite values. No bound on the sum of `vel_count` on one device may be relied on, other than what follows from the above.
Results may differ from a plain program's by a relative error of at most 0.0026.
Values may be sent and summed in bfloat16 or wider, within the bound.
A program may use at most 128 MiB of HBM per device.

v0:
```python
import functools

import jax
import jax.numpy as jnp
from jax import lax
from jax.experimental import pallas as pl
from jax.experimental.pallas import tpu as pltpu
from jax.sharding import PartitionSpec as P

SMAX = 16
LANES = 128
HALO = 16
EDGE = 8
PSF_ROW = 8
SMALL_ROWS = 16
MESH = pl.DeviceIdType.MESH
VMEM = pltpu.VMEM
SMEM = pltpu.SMEM

VIS, VIS_UP, VIS_DOWN, INV, SMALL, SMALL_UP, SMALL_DOWN, T_TOP, T_BOT, WEIGHT, F_TOP, F_BOT = range(12)
KINDS = 12


def split(value):
    high = value.astype(jnp.bfloat16)
    return high, (value - high.astype(jnp.float32)).astype(jnp.bfloat16)


def filter_kernel(
    tiles, epochs, ntaps, ftaps,
    visits, template, row_taps, col_taps, small, inv_var,
    win, norm,
    tbuf, xhigh, xlow, amat, vis, inv, whole, sbuf, rows_v, cols_v, gmat, diff, wbuf,
    send, recv, local,
):
    t = lax.axis_index("sky")
    e = lax.axis_index("epoch")
    height, width = visits.shape[1], visits.shape[2]
    band = template.shape[0]
    half = (ntaps - 1) // 2
    fhalf = (ftaps - 1) // 2
    last = epochs - 1
    has_up, has_down = t > 0, t < tiles - 1
    has_prev = jnp.logical_or(has_up, e > 0)
    has_next = jnp.logical_or(has_down, e < last)
    prev = (jnp.where(e > 0, t, t - 1), jnp.where(e > 0, e - 1, last))
    following = (jnp.where(e < last, t, t + 1), jnp.where(e < last, e + 1, 0))

    def span(owner):
        begin = max(0, owner * band - EDGE)
        end = min(height, owner * band + band + EDGE)
        return begin, end - begin, begin - (owner * band - EDGE)

    barrier = pltpu.get_barrier_semaphore()

    def greet(row, col):
        pl.semaphore_signal(barrier, inc=1, device_id=(row, col), device_id_type=MESH)

    for other in range(epochs):
        pl.when(e != other)(lambda other=other: greet(t, other))
        pl.when(has_up)(lambda other=other: greet(t - 1, other))
        pl.when(has_down)(lambda other=other: greet(t + 1, other))

    def near(src, dst, at):
        return pltpu.make_async_copy(src, dst, local.at[at])

    mid_t = tbuf.at[pl.ds(HALO, band)]
    near_t = near(template, mid_t, 0)
    near_rows = near(row_taps, rows_v, 1)
    near_cols = near(col_taps, cols_v, 2)
    near_small = near(small, sbuf.at[0, e], 3)
    near_whole = near(inv_var.at[0], whole, 4)

    def near_vis(owner):
        begin, count, to = span(owner)
        return near(visits.at[0, pl.ds(begin, count)], vis.at[owner, pl.ds(to, count)], 5)

    near_t.start()
    near_rows.start()
    near_cols.start()
    near_small.start()
    near_whole.start()
    for owner in range(epochs):
        pl.when(e == owner)(lambda owner=owner: near_vis(owner).start())

    def move(src, dst, kind, send_at, recv_at, where):
        return pltpu.make_async_remote_copy(
            src_ref=src, dst_ref=dst, send_sem=send.at[kind, send_at], recv_sem=recv.at[kind, recv_at],
            device_id=where, device_id_type=MESH,
        )

    def move_vis(owner, source):
        begin, count, to = span(owner)
        return move(visits.at[0, pl.ds(begin, count)], vis.at[source, pl.ds(to, count)], VIS, owner, source, (t, owner))

    def move_inv(owner, source):
        return move(inv_var.at[0, pl.ds(owner * band, band)], inv.at[source], INV, owner, source, (t, owner))

    tall = band + 2 * HALO
    outs = band + 2 * EDGE
    first = [
        (has_next, lambda: move(
            template.at[pl.ds(band - HALO, HALO)], tbuf.at[pl.ds(0, HALO)], T_TOP, 0, 0, following)),
        (has_prev, lambda: move(
            template.at[pl.ds(0, HALO)], tbuf.at[pl.ds(HALO + band, HALO)], T_BOT, 0, 0, prev)),
        (has_down, lambda: move(small, sbuf.at[1, e], SMALL_UP, 0, e, (t + 1, 0))),
        (has_up, lambda: move(small, sbuf.at[2, e], SMALL_DOWN, 0, e, (t - 1, last))),
    ]
    for other in range(epochs):
        first.append((e != other, lambda other=other: move(
            small, sbuf.at[0, e], SMALL, other, e, (t, other))))
    first.append((has_down, lambda: move(
        visits.at[0, pl.ds(height - EDGE, EDGE)], vis.at[e, pl.ds(0, EDGE)], VIS_UP, 0, e, (t + 1, 0))))
    first.append((has_up, lambda: move(
        visits.at[0, pl.ds(0, EDGE)], vis.at[e, pl.ds(outs - EDGE, EDGE)], VIS_DOWN, 0, e, (t - 1, last))))
    for other in range(epochs):
        first.append((e != other, lambda other=other: move_vis(other, e)))
    for other in range(epochs):
        first.append((e != other, lambda other=other: move_inv(other, e)))

    ups = jnp.where(has_up, epochs, 0)
    downs = jnp.where(has_down, epochs, 0)
    pl.semaphore_wait(barrier, epochs - 1 + ups + downs)
    for cond, make in first:
        pl.when(cond)(lambda make=make: make().start())

    def shifted_rows(start, count):
        body = tbuf[pl.ds(start, count), :]
        zeros = jnp.zeros((count, LANES), jnp.float32)
        high, low = split(jnp.concatenate([zeros, body, zeros], axis=1))
        for tap in range(ntaps):
            begin = LANES + tap - half
            xhigh[tap, pl.ds(start, count), :] = high[:, begin:begin + width]
            xlow[tap, pl.ds(start, count), :] = low[:, begin:begin + width]

    depth = xhigh.shape[1]
    if depth > tall:
        blank = jnp.zeros((depth - tall, width), jnp.bfloat16)
        for tap in range(ntaps):
            xhigh[tap, tall:depth, :] = blank
            xlow[tap, tall:depth, :] = blank

    near_t.wait()

    def shift_step(i, carry):
        shifted_rows(pl.multiple_of(HALO + i * 16, 16), 16)
        return carry

    lax.fori_loop(0, band // 16, shift_step, 0)

    near_small.wait()
    near_whole.wait()
    own_psf = sbuf[0, pl.ds(e, 1), PSF_ROW:PSF_ROW + 1, :]
    psf_power = jnp.sum(own_psf * own_psf)
    mean = jnp.sum(whole[...]) / (height * width)
    wbuf[pl.ds(e, 1)] = jnp.full((1, 8, LANES), psf_power * psf_power * mean, jnp.float32)
    inv[pl.ds(e, 1)] = whole[pl.ds(pl.multiple_of(e * band, 8), band), :][None]
    weights = []
    for other in range(epochs):
        weights.append((e != other, lambda other=other: move(
            wbuf.at[e], wbuf.at[e], WEIGHT, other, e, (t, other))))
    for cond, make in weights:
        pl.when(cond)(lambda make=make: make().start())

    near_rows.wait()
    near_cols.wait()
    for source in range(epochs):
        pl.when(e != source)(lambda source=source: move(
            small, sbuf.at[0, source], SMALL, source, source, (t, source)).wait_recv())
    for place, kind, at_end, exists in ((1, SMALL_UP, e == 0, has_up), (2, SMALL_DOWN, e == last, has_down)):
        @pl.when(jnp.logical_not(at_end))
        def _(place=place):
            sbuf[place] = sbuf[0]

        @pl.when(jnp.logical_and(at_end, jnp.logical_not(exists)))
        def _(place=place):
            sbuf[place] = jnp.zeros(sbuf.shape[1:], jnp.float32)

        for source in range(epochs):
            pl.when(jnp.logical_and(at_end, exists))(lambda place=place, kind=kind, source=source: move(
                small, sbuf.at[place, source], kind, 0, source, (t, e)).wait_recv())
    pad_taps = cols_v.shape[0]
    mixed = [
        cols_v[...] * sbuf[place, source, term:term + 1, :]
        for source in range(epochs) for place in range(3) for term in range(3)
    ]
    gmat[...] = jnp.dot(
        jnp.concatenate(mixed, axis=0), rows_v[...],
        precision=lax.Precision.HIGHEST, preferred_element_type=jnp.float32)

    row_iota = lax.broadcasted_iota(jnp.int32, (outs, 1), 0)
    in_tile = lax.rem(row_iota + (e * band + height - EDGE), height).astype(jnp.float32)
    centre = (height - 1) / 2.0
    w = (in_tile - centre) / centre
    total_rows = epochs * 2 * outs
    for source in range(epochs):
        for tap in range(ntaps):
            def base(term):
                def one(place, count):
                    at = ((source * 3 + place) * 3 + term) * pad_taps + tap
                    return jnp.broadcast_to(gmat[at:at + 1, :], (count, LANES))
                return jnp.concatenate([one(1, EDGE), one(0, band), one(2, EDGE)], axis=0)
            plain = pltpu.roll(base(0) + w * base(2), 0, 1, stride=1, stride_axis=0)
            slope = pltpu.roll(base(1), 0, 1, stride=1, stride_axis=0)
            high, low = split(jnp.concatenate([plain, slope], axis=0))
            at = source * 2 * outs
            amat[at:at + 2 * outs, tap * depth:(tap + 1) * depth] = high
            amat[total_rows + at:total_rows + at + 2 * outs, tap * depth:(tap + 1) * depth] = low

    @pl.when(jnp.logical_not(has_prev))
    def _():
        tbuf[0:HALO] = jnp.zeros((HALO, width), jnp.float32)
        for source in range(epochs):
            vis[source, 0:EDGE] = jnp.zeros((EDGE, width), jnp.float32)

    @pl.when(jnp.logical_not(has_next))
    def _():
        tbuf[HALO + band:tall] = jnp.zeros((HALO, width), jnp.float32)
        for source in range(epochs):
            vis[source, outs - EDGE:outs] = jnp.zeros((EDGE, width), jnp.float32)

    pl.when(has_prev)(lambda: move(
        template.at[pl.ds(0, HALO)], tbuf.at[pl.ds(0, HALO)], T_TOP, 0, 0, prev).wait_recv())
    pl.when(has_next)(lambda: move(
        template.at[pl.ds(0, HALO)], tbuf.at[pl.ds(HALO + band, HALO)], T_BOT, 0, 0, following).wait_recv())
    shifted_rows(0, HALO)
    shifted_rows(HALO + band, HALO)

    chunk = 256
    middle = (width - 1) / 2.0
    for col in range(0, width, chunk):
        here = slice(col, col + chunk)
        rhs_high = xhigh[:, :, here].reshape(ntaps * depth, chunk)
        rhs_low = xlow[:, :, here].reshape(ntaps * depth, chunk)
        big = jnp.dot(amat[...], rhs_high, preferred_element_type=jnp.float32)
        low = jnp.dot(amat[0:total_rows], rhs_low, preferred_element_type=jnp.float32)
        both = big[0:total_rows] + (big[total_rows:] + low)
        place = (lax.broadcasted_iota(jnp.int32, (1, chunk), 1) + col).astype(jnp.float32)
        u = (place - middle) / middle
        for source in range(epochs):
            at = source * 2 * outs
            diff[source, :, here] = both[at:at + outs] + u * both[at + outs:at + 2 * outs]

    for owner in range(epochs):
        @pl.when(e == owner)
        def _(owner=owner):
            near_vis(owner).wait()
            for source in range(epochs):
                if source != owner:
                    move_vis(owner, source).wait_recv()
    for source in range(epochs):
        pl.when(jnp.logical_and(e == 0, has_up))(lambda source=source: move(
            visits.at[0, pl.ds(0, EDGE)], vis.at[source, pl.ds(0, EDGE)], VIS_UP, 0, source, (t, e)).wait_recv())
        pl.when(jnp.logical_and(e == last, has_down))(lambda source=source: move(
            visits.at[0, pl.ds(0, EDGE)], vis.at[source, pl.ds(outs - EDGE, EDGE)], VIS_DOWN, 0, source,
            (t, e)).wait_recv())
    for source in range(epochs):
        diff[source] = vis[source] - diff[source]

    @pl.when(jnp.logical_not(has_prev))
    def _():
        for source in range(epochs):
            diff[source, 0:EDGE] = jnp.zeros((EDGE, width), jnp.float32)

    @pl.when(jnp.logical_not(has_next))
    def _():
        for source in range(epochs):
            diff[source, outs - EDGE:outs] = jnp.zeros((EDGE, width), jnp.float32)

    step = 16
    for source in range(epochs):
        pl.when(e != source)(lambda source=source: move(
            inv_var.at[0, pl.ds(0, band)], inv.at[source], INV, source, source, (t, source)).wait_recv())
        psf = [sbuf[0, source, PSF_ROW:PSF_ROW + 1, k:k + 1] for k in range(ftaps)]
        for start in range(0, band, step):
            total = None
            for k in range(ftaps):
                at = start + EDGE - fhalf + k
                term = psf[k] * diff[source, at:at + step, :]
                total = term if total is None else total + term
            zeros = jnp.zeros((step, LANES), jnp.float32)
            padded = jnp.concatenate([zeros, total, zeros], axis=1)
            smooth = None
            for k in range(ftaps):
                begin = LANES + k - fhalf
                term = psf[k] * padded[:, begin:begin + width]
                smooth = term if smooth is None else smooth + term
            win[source, SMAX + start:SMAX + start + step, :] = (
                smooth * inv[source, start:start + step, :]).astype(jnp.bfloat16)

    second = [
        (has_next, lambda: move(
            win.at[:, pl.ds(band, SMAX)], win.at[:, pl.ds(0, SMAX)], F_TOP, 0, 0, following)),
        (has_prev, lambda: move(
            win.at[:, pl.ds(SMAX, SMAX)], win.at[:, pl.ds(SMAX + band, SMAX)], F_BOT, 0, 0, prev)),
    ]
    for cond, make in second:
        pl.when(cond)(lambda make=make: make().start())

    @pl.when(jnp.logical_not(has_prev))
    def _():
        win[:, 0:SMAX, :] = jnp.zeros((epochs, SMAX, width), jnp.bfloat16)

    @pl.when(jnp.logical_not(has_next))
    def _():
        win[:, SMAX + band:, :] = jnp.zeros((epochs, SMAX, width), jnp.bfloat16)

    for source in range(epochs):
        pl.when(e != source)(lambda source=source: move(
            wbuf.at[source], wbuf.at[source], WEIGHT, source, source, (t, source)).wait_recv())
    norm[...] = jnp.sqrt(jnp.sum(wbuf[...], axis=0))
    for cond, make in first + weights:
        pl.when(cond)(lambda make=make: make().wait_send())
    pl.when(has_prev)(lambda: move(
        win.at[:, pl.ds(0, SMAX)], win.at[:, pl.ds(0, SMAX)], F_TOP, 0, 0, prev).wait_recv())
    pl.when(has_next)(lambda: move(
        win.at[:, pl.ds(0, SMAX)], win.at[:, pl.ds(SMAX + band, SMAX)], F_BOT, 0, 0, following).wait_recv())
    for cond, make in second:
        pl.when(cond)(lambda make=make: make().wait_send())


def search_kernel(epochs, win, norm, shifts, count, best, wide):
    band, width = best.shape
    rows = win.shape[1]
    parts = width // LANES

    def widen(i, carry):
        at = pl.multiple_of(i * 16, 16)
        for epoch in range(epochs):
            body = win[epoch, pl.ds(at, 16), :].astype(jnp.float32)
            padded = jnp.concatenate([body, jnp.zeros((16, LANES), jnp.float32)], axis=1)
            padded = pltpu.roll(padded, SMAX, 1)
            for part in range(parts + 1):
                wide[epoch, part, pl.ds(at, 16), :] = padded[:, part * LANES:(part + 1) * LANES]
        return carry

    lax.fori_loop(0, rows // 16, widen, 0)
    step = 16
    lane = lax.broadcasted_iota(jnp.int32, (step, LANES), 1)

    def stack(vel, finish):
        places = []
        for epoch in range(epochs):
            right = shifts[0, vel, epoch, 1] + SMAX
            places.append((
                shifts[0, vel, epoch, 0] + SMAX, lax.rem(LANES - right, LANES), lane < LANES - right))
        for start in range(0, band, step):
            sums = [None] * parts
            for epoch in range(epochs):
                down, turn, inside = places[epoch]
                turned = [
                    pltpu.roll(wide[epoch, part, pl.ds(start + down, step), :], turn, 1)
                    for part in range(parts + 1)
                ]
                for part in range(parts):
                    piece = jnp.where(inside, turned[part], turned[part + 1])
                    sums[part] = piece if sums[part] is None else sums[part] + piece
            for part in range(parts):
                finish((slice(start, start + step), slice(part * LANES, (part + 1) * LANES)), sums[part])

    def put(at, value):
        best[at] = value

    def raise_to(at, value):
        best[at] = jnp.maximum(best[at], value)

    def visit(vel, carry):
        stack(vel, raise_to)
        return carry

    stack(0, put)
    lax.fori_loop(1, count[0], visit, 0)
    best[...] = jnp.maximum(best[...] / norm[0:1, 0:1], -1e30)


def on_device(tiles, epochs, visits, template, basis_taps, coeffs, psf_taps, inv_var, shifts, vel_count):
    height, width = visits.shape[1], visits.shape[2]
    band = template.shape[0]
    nb, ntaps = basis_taps.shape[1], basis_taps.shape[2]
    ftaps = psf_taps.shape[1]
    pad_taps = -(-ntaps // 8) * 8
    tall = band + 2 * HALO
    outs = band + 2 * EDGE
    depth = LANES
    assert tall <= depth and nb <= LANES and band >= HALO and outs - 1 + ntaps <= depth

    row_taps = jnp.pad(basis_taps[0], ((0, LANES - nb), (0, LANES - ntaps)))
    col_taps = jnp.pad(basis_taps[1].T, ((0, pad_taps - ntaps), (0, LANES - nb)))
    terms = coeffs.shape[3]
    small = jnp.concatenate([
        jnp.pad(coeffs[0, 0].T, ((0, PSF_ROW - terms), (0, LANES - nb))),
        jnp.pad(psf_taps, ((0, SMALL_ROWS - PSF_ROW - 1), (0, LANES - ftaps))),
    ], axis=0)

    vmem = pl.BlockSpec(memory_space=VMEM)
    smem = pl.BlockSpec(memory_space=SMEM)
    hbm = pl.BlockSpec(memory_space=pltpu.HBM)
    win, norm = pl.pallas_call(
        functools.partial(filter_kernel, tiles, epochs, ntaps, ftaps),
        out_shape=(
            jax.ShapeDtypeStruct((epochs, band + 2 * SMAX, width), jnp.bfloat16),
            jax.ShapeDtypeStruct((8, LANES), jnp.float32),
        ),
        in_specs=[hbm] * 6,
        out_specs=(vmem, vmem),
        scratch_shapes=[
            VMEM((tall, width), jnp.float32),
            VMEM((ntaps, depth, width), jnp.bfloat16),
            VMEM((ntaps, depth, width), jnp.bfloat16),
            VMEM((2 * epochs * 2 * outs, ntaps * depth), jnp.bfloat16),
            VMEM((epochs, outs, width), jnp.float32),
            VMEM((epochs, band, width), jnp.float32),
            VMEM((height, width), jnp.float32),
            VMEM((3, epochs, SMALL_ROWS, LANES), jnp.float32),
            VMEM((LANES, LANES), jnp.float32),
            VMEM((pad_taps, LANES), jnp.float32),
            VMEM((epochs * 9 * pad_taps, LANES), jnp.float32),
            VMEM((epochs, outs, width), jnp.float32),
            VMEM((epochs, 8, LANES), jnp.float32),
            pltpu.SemaphoreType.DMA((KINDS, epochs)),
            pltpu.SemaphoreType.DMA((KINDS, epochs)),
            pltpu.SemaphoreType.DMA((6,)),
        ],
        compiler_params=pltpu.CompilerParams(
            collective_id=0, has_side_effects=True, vmem_limit_bytes=40 * 1024 * 1024),
        name="filter",
    )(visits, template, row_taps, col_taps, small, inv_var)
    return pl.pallas_call(
        functools.partial(search_kernel, epochs),
        out_shape=jax.ShapeDtypeStruct((band, width), jnp.float32),
        in_specs=[vmem, vmem, smem, smem],
        out_specs=vmem,
        scratch_shapes=[VMEM((epochs, width // LANES + 1, band + 2 * SMAX, LANES), jnp.float32)],
        compiler_params=pltpu.CompilerParams(vmem_limit_bytes=24 * 1024 * 1024),
        name="search",
    )(win, norm, shifts, vel_count)


def solution(mesh):
    in_specs = (
        P("epoch", "sky", None),
        P(("sky", "epoch"), None),
        P(),
        P("epoch", "sky", None, None),
        P("epoch", None),
        P("epoch", "sky", None),
        P("sky", None, None, None),
        P("sky"),
    )
    body = functools.partial(on_device, mesh.shape["sky"], mesh.shape["epoch"])
    return jax.shard_map(
        body, mesh=mesh, in_specs=in_specs, out_specs=P(("sky", "epoch"), None), check_vma=False)
```

profile of v0, /device:TPU:25, one launch (start us, length us, event | category | flops | bytes accessed | tf_op | source)
XLA Modules:
  0.0 39.8 jit_solution(5397294047675763638)
XLA Ops:
  0.0 0.0 copy-start.3
  0.7 0.7 %copy.18 = f32[1,1,27,3]{2,3,1,0:T(4,128)S(1)} copy(f32[1,1,27,3]{2,1,3,0:T(1,128)} %param.11) | data formatting | bytes 648
  1.3 0.7 %select_maximum_fusion.small = f32[16,128]{1,0:T(8,128)S(1)} fusion(f32[1,9]{1,0:T(1,128)} %param.12, f32[3,27]{1,0:T(4,128)S(1)} %bitcast.13), kind=kLoop, calls=%fused_computation.1 | loop fusion | flops 10240 | bytes 8552 | tf_op jit(solution)/shard_map/concatenate | solution.py:390
  2.0 0.0 copy-done.3
  2.1 0.0 copy-start.4
  2.1 0.1 copy.13
  2.2 0.6 %copy-done.4 = s32[1,24,2,2]{1,3,2,0:T(2,128)S(1)} copy-done((s32[1,24,2,2]{1,3,2,0:T(2,128)S(1)}, s32[1,24,2,2]{1,3,2,0:T(2,128)}, u32[]{:S(2)}) %copy-start.4) | copy-done | bytes 408
  2.7 0.1 copy.11.shifts
  2.8 0.0 copy-start
  2.9 1.0 %copy-done = f32[1,128,1024]{2,1,0:T(8,128)S(1)} copy-done((f32[1,128,1024]{2,1,0:T(8,128)S(1)}, f32[1,128,1024]{2,1,0:T(8,128)}, u32[]{:S(2)}) %copy-start) | copy-done | bytes 524312
  3.9 0.0 copy-start.1
  3.9 1.0 %copy-done.1 = f32[1,128,1024]{2,1,0:T(8,128)S(1)} copy-done((f32[1,128,1024]{2,1,0:T(8,128)S(1)}, f32[1,128,1024]{2,1,0:T(8,128)}, u32[]{:S(2)}) %copy-start.1) | copy-done | bytes 524312
  4.9 0.0 copy-start.2
  4.9 0.9 %copy-done.2 = f32[64,1024]{1,0:T(8,128)S(1)} copy-done((f32[64,1024]{1,0:T(8,128)S(1)}, f32[64,1024]{1,0:T(8,128)}, u32[]{:S(2)}) %copy-start.2) | copy-done | bytes 262168
  5.9 26.2 %filter.1 = (bf16[2,96,1024]{2,1,0:T(8,128)(2,1)S(1)}, f32[8,128]{1,0:T(8,128)S(1)}) custom-call(f32[1,128,1024]{2,1,0:T(8,128)S(1)} %copy-done, f32[64,1024]{1,0:T(8,128)S(1)} %copy-done.2, f32[128,128]{1,0:T(8,128)S(1)} %pad.16.row_taps, f32[24,128]{1,0:T(8,128)S(1)} %pad.17.col_taps, f32[16,128]{1,0:T(8,128)S(1)} %select_maximum_fusion.small, ...), custom_call_target="tpu_custom_call" | custom-call | tf_op jit(solution)/shard_map/filter/pallas_call | solution.py:398
  32.1 7.7 %search.1 = f32[64,1024]{1,0:T(8,128)} custom-call(bf16[2,96,1024]{2,1,0:T(8,128)(2,1)S(1)} %get-tuple-element.7.win, f32[8,128]{1,0:T(8,128)S(1)} %get-tuple-element.8.norm, s32[1,24,2,2]{3,2,1,0:T(2,128)S(1)} %copy.11.shifts, s32[1]{0:T(128)S(6)} %copy.19.count), custom_call_target="tpu_custom_call" | custom-call | tf_op jit(solution)/shard_map/search/pallas_call | solution.py:428
  (4 shorter events, 0.0 us)
Async XLA Ops:
  0.0 2.0 %copy-start.3 = (f32[2,27,17]{1,0,2:T(2,128)S(1)}, f32[2,27,17]{1,0,2:T(2,128)}, u32[]{:S(2)}) copy-start(f32[2,27,17]{1,0,2:T(2,128)} %param.10) | copy-start | bytes 11020
  2.1 0.7 %copy-start.4 = (s32[1,24,2,2]{1,3,2,0:T(2,128)S(1)}, s32[1,24,2,2]{1,3,2,0:T(2,128)}, u32[]{:S(2)}) copy-start(s32[1,24,2,2]{1,3,2,0:T(2,128)} %param.14) | copy-start | bytes 1156
  2.8 1.0 %copy-start = (f32[1,128,1024]{2,1,0:T(8,128)S(1)}, f32[1,128,1024]{2,1,0:T(8,128)}, u32[]{:S(2)}) copy-start(f32[1,128,1024]{2,1,0:T(8,128)} %visits.1) | copy-start | bytes 1572868
  3.9 1.0 %copy-start.1 = (f32[1,128,1024]{2,1,0:T(8,128)S(1)}, f32[1,128,1024]{2,1,0:T(8,128)}, u32[]{:S(2)}) copy-start(f32[1,128,1024]{2,1,0:T(8,128)} %inv_var.1) | copy-start | bytes 1572868
  4.9 0.9 %copy-start.2 = (f32[64,1024]{1,0:T(8,128)S(1)}, f32[64,1024]{1,0:T(8,128)}, u32[]{:S(2)}) copy-start(f32[64,1024]{1,0:T(8,128)} %template.1) | copy-start | bytes 786436
where the time goes:
time: 40.5 us; the launch traced here: 39.8 us
  Pallas kernels  34 us (84%)
  local copies, waits for them, and re-layouts  4.52 us (11%)
  between operations  0.71 us (2%)
  other arithmetic  0.66 us (2%)
    pallas_call x1, Pallas kernels, on_device(): pl.pallas_call(functools.partial(filter_kernel, tiles, epochs, ntaps, fta...  26.2 us
    pallas_call x1, Pallas kernels, on_device(): pl.pallas_call(functools.partial(search_kernel, epochs), out_shape=jax.Sh...  7.72 us
    unnamed x14, local copies, waits for them, and re-layouts  4.49 us

commit v1 on v0

--- a/solution.py
+++ b/solution.py
@@ -28,9 +28,9 @@
 
 def filter_kernel(
     tiles, epochs, ntaps, ftaps,
-    visits, template, row_taps, col_taps, small, inv_var,
-    win, norm,
-    tbuf, xhigh, xlow, amat, vis, inv, whole, sbuf, rows_v, cols_v, gmat, diff, wbuf,
+    visits, template, taps, coeffs, psf_taps, inv_var, shifts, count,
+    best,
+    win, wide, tbuf, xhigh, xlow, amat, vis, inv, whole, sbuf, rows_v, cols_v, gmat, diff, wbuf, taps_v, coeffs_v, psf_v,
     send, recv, local,
 ):
     t = lax.axis_index("sky")
@@ -66,19 +66,20 @@
 
     mid_t = tbuf.at[pl.ds(HALO, band)]
     near_t = near(template, mid_t, 0)
-    near_rows = near(row_taps, rows_v, 1)
-    near_cols = near(col_taps, cols_v, 2)
-    near_small = near(small, sbuf.at[0, e], 3)
+    near_taps = near(taps, taps_v, 1)
+    near_coeffs = near(coeffs, coeffs_v, 2)
+    near_psf = near(psf_taps, psf_v, 3)
+    small = sbuf.at[0, e]
     near_whole = near(inv_var.at[0], whole, 4)
 
     def near_vis(owner):
         begin, count, to = span(owner)
         return near(visits.at[0, pl.ds(begin, count)], vis.at[owner, pl.ds(to, count)], 5)
 
+    near_coeffs.start()
+    near_psf.start()
+    near_taps.start()
     near_t.start()
-    near_rows.start()
-    near_cols.start()
-    near_small.start()
     near_whole.start()
     for owner in range(epochs):
         pl.when(e == owner)(lambda owner=owner: near_vis(owner).start())
@@ -118,6 +119,16 @@
     for other in range(epochs):
         first.append((e != other, lambda other=other: move_inv(other, e)))
 
+    sbuf[0, pl.ds(e, 1)] = jnp.zeros((1, SMALL_ROWS, LANES), jnp.float32)
+    rows_v[...] = jnp.zeros(rows_v.shape, jnp.float32)
+    cols_v[...] = jnp.zeros(cols_v.shape, jnp.float32)
+    near_coeffs.wait()
+    near_psf.wait()
+    nb = taps.shape[2]
+    for term in range(coeffs.shape[0]):
+        sbuf[0, pl.ds(e, 1), term:term + 1, 0:nb] = coeffs_v[term][None]
+    sbuf[0, pl.ds(e, 1), PSF_ROW:PSF_ROW + 1, 0:ftaps] = psf_v[...][None]
+
     ups = jnp.where(has_up, epochs, 0)
     downs = jnp.where(has_down, epochs, 0)
     pl.semaphore_wait(barrier, epochs - 1 + ups + downs)
@@ -140,6 +151,10 @@
             xhigh[tap, tall:depth, :] = blank
             xlow[tap, tall:depth, :] = blank
 
+    near_taps.wait()
+    for tap in range(ntaps):
+        rows_v[tap:tap + 1, 0:nb] = taps_v[tap, 0:1, :]
+        cols_v[tap:tap + 1, 0:nb] = taps_v[tap, 1:2, :]
     near_t.wait()
 
     def shift_step(i, carry):
@@ -148,7 +163,6 @@
 
     lax.fori_loop(0, band // 16, shift_step, 0)
 
-    near_small.wait()
     near_whole.wait()
     own_psf = sbuf[0, pl.ds(e, 1), PSF_ROW:PSF_ROW + 1, :]
     psf_power = jnp.sum(own_psf * own_psf)
@@ -162,8 +176,6 @@
     for cond, make in weights:
         pl.when(cond)(lambda make=make: make().start())
 
-    near_rows.wait()
-    near_cols.wait()
     for source in range(epochs):
         pl.when(e != source)(lambda source=source: move(
             small, sbuf.at[0, source], SMALL, source, source, (t, source)).wait_recv())
@@ -184,8 +196,8 @@
         cols_v[...] * sbuf[place, source, term:term + 1, :]
         for source in range(epochs) for place in range(3) for term in range(3)
     ]
-    gmat[...] = jnp.dot(
-        jnp.concatenate(mixed, axis=0), rows_v[...],
+    gmat[...] = lax.dot_general(
+        jnp.concatenate(mixed, axis=0), rows_v[...], (((1,), (1,)), ((), ())),
         precision=lax.Precision.HIGHEST, preferred_element_type=jnp.float32)
 
     row_iota = lax.broadcasted_iota(jnp.int32, (outs, 1), 0)
@@ -267,16 +279,32 @@
         for source in range(epochs):
             diff[source, outs - EDGE:outs] = jnp.zeros((EDGE, width), jnp.float32)
 
+    @pl.when(jnp.logical_not(has_prev))
+    def _():
+        win[:, 0:SMAX, :] = jnp.zeros((epochs, SMAX, width), jnp.bfloat16)
+
+    @pl.when(jnp.logical_not(has_next))
+    def _():
+        win[:, SMAX + band:, :] = jnp.zeros((epochs, SMAX, width), jnp.bfloat16)
+
     step = 16
-    for source in range(epochs):
-        pl.when(e != source)(lambda source=source: move(
-            inv_var.at[0, pl.ds(0, band)], inv.at[source], INV, source, source, (t, source)).wait_recv())
-        psf = [sbuf[0, source, PSF_ROW:PSF_ROW + 1, k:k + 1] for k in range(ftaps)]
-        for start in range(0, band, step):
+    inner = list(range(0, band, step))
+    edges = sorted({inner[0], inner[-1]})
+    inner = [start for start in inner if start not in edges]
+    second = []
+    for turn in range(epochs):
+        source = lax.rem(e + turn, epochs)
+        if turn:
+            move(inv_var.at[0, pl.ds(0, band)], inv.at[source], INV, 0, source, (t, source)).wait_recv()
+        taps_row = sbuf[0, pl.ds(source, 1), PSF_ROW:PSF_ROW + 1, :][0]
+        psf = [jnp.broadcast_to(taps_row[:, k:k + 1], (8, LANES)) for k in range(ftaps)]
+        psf = [jnp.tile(value, (step // 8, width // LANES)) for value in psf]
+
+        def smooth_rows(start):
             total = None
             for k in range(ftaps):
                 at = start + EDGE - fhalf + k
-                term = psf[k] * diff[source, at:at + step, :]
+                term = psf[k] * diff[pl.ds(source, 1), at:at + step, :][0]
                 total = term if total is None else total + term
             zeros = jnp.zeros((step, LANES), jnp.float32)
             padded = jnp.concatenate([zeros, total, zeros], axis=1)
@@ -285,41 +313,42 @@
                 begin = LANES + k - fhalf
                 term = psf[k] * padded[:, begin:begin + width]
                 smooth = term if smooth is None else smooth + term
-            win[source, SMAX + start:SMAX + start + step, :] = (
-                smooth * inv[source, start:start + step, :]).astype(jnp.bfloat16)
-
-    second = [
-        (has_next, lambda: move(
-            win.at[:, pl.ds(band, SMAX)], win.at[:, pl.ds(0, SMAX)], F_TOP, 0, 0, following)),
-        (has_prev, lambda: move(
-            win.at[:, pl.ds(SMAX, SMAX)], win.at[:, pl.ds(SMAX + band, SMAX)], F_BOT, 0, 0, prev)),
-    ]
-    for cond, make in second:
-        pl.when(cond)(lambda make=make: make().start())
-
-    @pl.when(jnp.logical_not(has_prev))
-    def _():
-        win[:, 0:SMAX, :] = jnp.zeros((epochs, SMAX, width), jnp.bfloat16)
-
-    @pl.when(jnp.logical_not(has_next))
-    def _():
-        win[:, SMAX + band:, :] = jnp.zeros((epochs, SMAX, width), jnp.bfloat16)
+            value = (smooth * inv[pl.ds(source, 1), start:start + step, :][0]).astype(jnp.bfloat16)
+            win[pl.ds(source, 1), SMAX + start:SMAX + start + step, :] = value[None]
+
+        for start in edges:
+            smooth_rows(start)
+        pair = [
+            (has_next, lambda source=source: move(
+                win.at[source, pl.ds(band, SMAX)], win.at[source, pl.ds(0, SMAX)],
+                F_TOP, source, source, following)),
+            (has_prev, lambda source=source: move(
+                win.at[source, pl.ds(SMAX, SMAX)], win.at[source, pl.ds(SMAX + band, SMAX)],
+                F_BOT, source, source, prev)),
+        ]
+        for cond, make in pair:
+            pl.when(cond)(lambda make=make: make().start())
+        second += pair
+        for start in inner:
+            smooth_rows(start)
 
     for source in range(epochs):
         pl.when(e != source)(lambda source=source: move(
             wbuf.at[source], wbuf.at[source], WEIGHT, source, source, (t, source)).wait_recv())
-    norm[...] = jnp.sqrt(jnp.sum(wbuf[...], axis=0))
     for cond, make in first + weights:
         pl.when(cond)(lambda make=make: make().wait_send())
-    pl.when(has_prev)(lambda: move(
-        win.at[:, pl.ds(0, SMAX)], win.at[:, pl.ds(0, SMAX)], F_TOP, 0, 0, prev).wait_recv())
-    pl.when(has_next)(lambda: move(
-        win.at[:, pl.ds(0, SMAX)], win.at[:, pl.ds(SMAX + band, SMAX)], F_BOT, 0, 0, following).wait_recv())
+    for source in range(epochs):
+        pl.when(has_prev)(lambda source=source: move(
+            win.at[source, pl.ds(0, SMAX)], win.at[source, pl.ds(0, SMAX)], F_TOP, 0, source, prev).wait_recv())
+        pl.when(has_next)(lambda source=source: move(
+            win.at[source, pl.ds(0, SMAX)], win.at[source, pl.ds(SMAX + band, SMAX)],
+            F_BOT, 0, source, following).wait_recv())
+    search(epochs, win, jnp.sqrt(jnp.sum(wbuf[...], axis=0)), shifts, count, best, wide)
     for cond, make in second:
         pl.when(cond)(lambda make=make: make().wait_send())
 
 
-def search_kernel(epochs, win, norm, shifts, count, best, wide):
+def search(epochs, win, norm, shifts, count, best, wide):
     band, width = best.shape
     rows = win.shape[1]
     parts = width // LANES
@@ -338,38 +367,43 @@
     step = 16
     lane = lax.broadcasted_iota(jnp.int32, (step, LANES), 1)
 
-    def stack(vel, finish):
+    listed = count[0]
+    group = 4
+
+    def places_of(vel):
         places = []
         for epoch in range(epochs):
-            right = shifts[0, vel, epoch, 1] + SMAX
+            right = shifts[epoch, 1, vel] + SMAX
             places.append((
-                shifts[0, vel, epoch, 0] + SMAX, lax.rem(LANES - right, LANES), lane < LANES - right))
+                shifts[epoch, 0, vel] + SMAX, lax.rem(LANES - right, LANES), lane < LANES - right))
+        return places
+
+    def stack(places, start):
+        sums = [None] * parts
+        for epoch in range(epochs):
+            down, turn, inside = places[epoch]
+            turned = [
+                pltpu.roll(wide[epoch, part, pl.ds(start + down, step), :], turn, 1)
+                for part in range(parts + 1)
+            ]
+            for part in range(parts):
+                piece = jnp.where(inside, turned[part], turned[part + 1])
+                sums[part] = piece if sums[part] is None else sums[part] + piece
+        return sums
+
+    best[...] = jnp.full(best.shape, -jnp.inf, jnp.float32)
+
+    def visit(turn, carry):
+        every = [places_of(jnp.maximum(jnp.minimum(turn * group + i, listed - 1), 0)) for i in range(group)]
         for start in range(0, band, step):
-            sums = [None] * parts
-            for epoch in range(epochs):
-                down, turn, inside = places[epoch]
-                turned = [
-                    pltpu.roll(wide[epoch, part, pl.ds(start + down, step), :], turn, 1)
-                    for part in range(parts + 1)
-                ]
-                for part in range(parts):
-                    piece = jnp.where(inside, turned[part], turned[part + 1])
-                    sums[part] = piece if sums[part] is None else sums[part] + piece
+            top = [best[start:start + step, part * LANES:(part + 1) * LANES] for part in range(parts)]
+            for places in every:
+                top = [jnp.maximum(a, b) for a, b in zip(top, stack(places, start))]
             for part in range(parts):
-                finish((slice(start, start + step), slice(part * LANES, (part + 1) * LANES)), sums[part])
-
-    def put(at, value):
-        best[at] = value
-
-    def raise_to(at, value):
-        best[at] = jnp.maximum(best[at], value)
-
-    def visit(vel, carry):
-        stack(vel, raise_to)
+                best[start:start + step, part * LANES:(part + 1) * LANES] = top[part]
         return carry
 
-    stack(0, put)
-    lax.fori_loop(1, count[0], visit, 0)
+    lax.fori_loop(0, -(-shifts.shape[2] // group), visit, 0)
     best[...] = jnp.maximum(best[...] / norm[0:1, 0:1], -1e30)
 
 
@@ -384,26 +418,20 @@
     depth = LANES
     assert tall <= depth and nb <= LANES and band >= HALO and outs - 1 + ntaps <= depth
 
-    row_taps = jnp.pad(basis_taps[0], ((0, LANES - nb), (0, LANES - ntaps)))
-    col_taps = jnp.pad(basis_taps[1].T, ((0, pad_taps - ntaps), (0, LANES - nb)))
-    terms = coeffs.shape[3]
-    small = jnp.concatenate([
-        jnp.pad(coeffs[0, 0].T, ((0, PSF_ROW - terms), (0, LANES - nb))),
-        jnp.pad(psf_taps, ((0, SMALL_ROWS - PSF_ROW - 1), (0, LANES - ftaps))),
-    ], axis=0)
-
+    taps = jnp.transpose(basis_taps, (2, 0, 1))
+    terms = jnp.transpose(coeffs[0], (2, 0, 1))
+    listed = jnp.transpose(shifts[0], (1, 2, 0))
     vmem = pl.BlockSpec(memory_space=VMEM)
     smem = pl.BlockSpec(memory_space=SMEM)
     hbm = pl.BlockSpec(memory_space=pltpu.HBM)
-    win, norm = pl.pallas_call(
+    return pl.pallas_call(
         functools.partial(filter_kernel, tiles, epochs, ntaps, ftaps),
-        out_shape=(
-            jax.ShapeDtypeStruct((epochs, band + 2 * SMAX, width), jnp.bfloat16),
-            jax.ShapeDtypeStruct((8, LANES), jnp.float32),
-        ),
-        in_specs=[hbm] * 6,
-        out_specs=(vmem, vmem),
+        out_shape=jax.ShapeDtypeStruct((band, width), jnp.float32),
+        in_specs=[hbm] * 6 + [smem] * 2,
+        out_specs=vmem,
         scratch_shapes=[
+            VMEM((epochs, band + 2 * SMAX, width), jnp.bfloat16),
+            VMEM((epochs, width // LANES + 1, band + 2 * SMAX, LANES), jnp.float32),
             VMEM((tall, width), jnp.float32),
             VMEM((ntaps, depth, width), jnp.bfloat16),
             VMEM((ntaps, depth, width), jnp.bfloat16),
@@ -417,23 +445,17 @@
             VMEM((epochs * 9 * pad_taps, LANES), jnp.float32),
             VMEM((epochs, outs, width), jnp.float32),
             VMEM((epochs, 8, LANES), jnp.float32),
+            VMEM(taps.shape, jnp.float32),
+            VMEM(terms.shape, jnp.float32),
+            VMEM(psf_taps.shape, jnp.float32),
             pltpu.SemaphoreType.DMA((KINDS, epochs)),
             pltpu.SemaphoreType.DMA((KINDS, epochs)),
             pltpu.SemaphoreType.DMA((6,)),
         ],
         compiler_params=pltpu.CompilerParams(
-            collective_id=0, has_side_effects=True, vmem_limit_bytes=40 * 1024 * 1024),
-        name="filter",
-    )(visits, template, row_taps, col_taps, small, inv_var)
-    return pl.pallas_call(
-        functools.partial(search_kernel, epochs),
-        out_shape=jax.ShapeDtypeStruct((band, width), jnp.float32),
-        in_specs=[vmem, vmem, smem, smem],
-        out_specs=vmem,
-        scratch_shapes=[VMEM((epochs, width // LANES + 1, band + 2 * SMAX, LANES), jnp.float32)],
-        compiler_params=pltpu.CompilerParams(vmem_limit_bytes=24 * 1024 * 1024),
-        name="search",
-    )(win, norm, shifts, vel_count)
+            collective_id=0, has_side_effects=True, vmem_limit_bytes=60 * 1024 * 1024),
+        name="detect",
+    )(visits, template, taps, terms, psf_taps, inv_var, listed, vel_count)
 
 
 def solution(mesh):

time: 40.5 us -> 34 us (0.84)
  the two profiles are of different devices: /device:TPU:25 before, /device:TPU:17 now
where the time goes in v1:
time: 34 us; the launch traced here: 33.3 us
  Pallas kernels  31 us (91%)
  local copies, waits for them, and re-layouts  1.67 us (5%)
  between operations  0.66 us (2%)
    pallas_call x1, Pallas kernels, on_device(): pl.pallas_call(functools.partial(filter_kernel, tiles, epochs, ntaps, fta...  31 us
    unnamed x1, local copies, waits for them, and re-layouts  1.67 us

profile of v1, /device:TPU:17, one launch (start us, length us, event | category | flops | bytes accessed | tf_op | source)
XLA Modules:
  0.0 33.3 jit_solution(5101376067558331694)
XLA Ops:
  0.7 31.0 %detect.1 = f32[64,1024]{1,0:T(8,128)} custom-call(f32[1,128,1024]{2,1,0:T(8,128)} %visits.1, f32[64,1024]{1,0:T(8,128)} %template.1, f32[17,2,27]{2,1,0:T(2,128)} %bitcast.7, f32[3,1,27]{2,1,0:T(1,128)} %bitcast.9, f32[1,9]{1,0:T(1,128)} %psf_taps.1, f32[1,128,1024]{2,1,0:T(8,128)} %inv_var.1, s32[2,2,24]{2,1,0:T(2,128)} %bitcast.8, s32[1]{0:T(128)S(6)} %copy.10.count), custom_call_target="tpu_custom_call" | custom-call | tf_op jit(solution)/shard_map/detect/pallas_call | solution.py:427
  31.6 1.7 %copy.11 = f32[64,1024]{1,0:T(8,128)} copy(f32[64,1024]{1,0:T(8,128)} %detect.1) | data formatting | bytes 524288

commit v2 on v1

--- a/solution.py
+++ b/solution.py
@@ -145,23 +145,14 @@
             xlow[tap, pl.ds(start, count), :] = low[:, begin:begin + width]
 
     depth = xhigh.shape[1]
-    if depth > tall:
-        blank = jnp.zeros((depth - tall, width), jnp.bfloat16)
-        for tap in range(ntaps):
-            xhigh[tap, tall:depth, :] = blank
-            xlow[tap, tall:depth, :] = blank
-
     near_taps.wait()
     for tap in range(ntaps):
         rows_v[tap:tap + 1, 0:nb] = taps_v[tap, 0:1, :]
         cols_v[tap:tap + 1, 0:nb] = taps_v[tap, 1:2, :]
     near_t.wait()
 
-    def shift_step(i, carry):
-        shifted_rows(pl.multiple_of(HALO + i * 16, 16), 16)
-        return carry
-
-    lax.fori_loop(0, band // 16, shift_step, 0)
+    for start in range(HALO, HALO + band, 16):
+        shifted_rows(start, 16)
 
     near_whole.wait()
     own_psf = sbuf[0, pl.ds(e, 1), PSF_ROW:PSF_ROW + 1, :]
@@ -216,8 +207,8 @@
             slope = pltpu.roll(base(1), 0, 1, stride=1, stride_axis=0)
             high, low = split(jnp.concatenate([plain, slope], axis=0))
             at = source * 2 * outs
-            amat[at:at + 2 * outs, tap * depth:(tap + 1) * depth] = high
-            amat[total_rows + at:total_rows + at + 2 * outs, tap * depth:(tap + 1) * depth] = low
+            amat[at:at + 2 * outs, tap * depth:(tap + 1) * depth] = high[:, 0:depth]
+            amat[total_rows + at:total_rows + at + 2 * outs, tap * depth:(tap + 1) * depth] = low[:, 0:depth]
 
     @pl.when(jnp.logical_not(has_prev))
     def _():
@@ -332,6 +323,8 @@
         for start in inner:
             smooth_rows(start)
 
+    for start in range(SMAX, SMAX + band, 16):
+        widen(win, wide, start)
     for source in range(epochs):
         pl.when(e != source)(lambda source=source: move(
             wbuf.at[source], wbuf.at[source], WEIGHT, source, source, (t, source)).wait_recv())
@@ -343,27 +336,27 @@
         pl.when(has_next)(lambda source=source: move(
             win.at[source, pl.ds(0, SMAX)], win.at[source, pl.ds(SMAX + band, SMAX)],
             F_BOT, 0, source, following).wait_recv())
-    search(epochs, win, jnp.sqrt(jnp.sum(wbuf[...], axis=0)), shifts, count, best, wide)
+    widen(win, wide, 0)
+    widen(win, wide, SMAX + band)
+    search(epochs, jnp.sqrt(jnp.sum(wbuf[...], axis=0)), shifts, count, best, wide)
     for cond, make in second:
         pl.when(cond)(lambda make=make: make().wait_send())
 
 
-def search(epochs, win, norm, shifts, count, best, wide):
+def widen(win, wide, at):
+    parts = win.shape[2] // LANES
+    for epoch in range(win.shape[0]):
+        body = win[epoch, at:at + 16, :].astype(jnp.float32)
+        padded = jnp.concatenate([body, jnp.zeros((16, LANES), jnp.float32)], axis=1)
+        padded = pltpu.roll(padded, SMAX, 1)
+        for part in range(parts + 1):
+            wide[epoch, part, at:at + 16, :] = padded[:, part * LANES:(part + 1) * LANES]
+
+
+def search(epochs, norm, shifts, count, best, wide):
     band, width = best.shape
-    rows = win.shape[1]
     parts = width // LANES
 
-    def widen(i, carry):
-        at = pl.multiple_of(i * 16, 16)
-        for epoch in range(epochs):
-            body = win[epoch, pl.ds(at, 16), :].astype(jnp.float32)
-            padded = jnp.concatenate([body, jnp.zeros((16, LANES), jnp.float32)], axis=1)
-            padded = pltpu.roll(padded, SMAX, 1)
-            for part in range(parts + 1):
-                wide[epoch, part, pl.ds(at, 16), :] = padded[:, part * LANES:(part + 1) * LANES]
-        return carry
-
-    lax.fori_loop(0, rows // 16, widen, 0)
     step = 16
     lane = lax.broadcasted_iota(jnp.int32, (step, LANES), 1)
 
@@ -415,8 +408,8 @@
     pad_taps = -(-ntaps // 8) * 8
     tall = band + 2 * HALO
     outs = band + 2 * EDGE
-    depth = LANES
-    assert tall <= depth and nb <= LANES and band >= HALO and outs - 1 + ntaps <= depth
+    depth = tall
+    assert tall <= LANES and nb <= LANES and band >= HALO and outs - 1 + ntaps <= depth
 
     taps = jnp.transpose(basis_taps, (2, 0, 1))
     terms = jnp.transpose(coeffs[0], (2, 0, 1))

time: 34 us -> 33.5 us (0.985)
  Pallas kernels: 31 us -> 30.6 us
    pallas_call x1, Pallas kernels: 31 us -> 30.6 us  [on_device(): pl.pallas_call(functools.partial(filter_kernel, tiles, epochs, ntaps, fta...]
where the time goes in v2:
time: 33.5 us; the launch traced here: 32.9 us
  Pallas kernels  30.6 us (91%)
  local copies, waits for them, and re-layouts  1.67 us (5%)
  between operations  0.66 us (2%)
    pallas_call x1, Pallas kernels, on_device(): pl.pallas_call(functools.partial(filter_kernel, tiles, epochs, ntaps, fta...  30.6 us
    unnamed x1, local copies, waits for them, and re-layouts  1.67 us

profile of v2, /device:TPU:17, one launch (start us, length us, event | category | flops | bytes accessed | tf_op | source)
XLA Modules:
  0.0 32.9 jit_solution(15325766506877229712)
XLA Ops:
  0.7 30.6 %detect.1 = f32[64,1024]{1,0:T(8,128)} custom-call(f32[1,128,1024]{2,1,0:T(8,128)} %visits.1, f32[64,1024]{1,0:T(8,128)} %template.1, f32[17,2,27]{2,1,0:T(2,128)} %bitcast.7, f32[3,1,27]{2,1,0:T(1,128)} %bitcast.9, f32[1,9]{1,0:T(1,128)} %psf_taps.1, f32[1,128,1024]{2,1,0:T(8,128)} %inv_var.1, s32[2,2,24]{2,1,0:T(2,128)} %bitcast.8, s32[1]{0:T(128)S(6)} %copy.10.count), custom_call_target="tpu_custom_call" | custom-call | tf_op jit(solution)/shard_map/detect/pallas_call | solution.py:420
  31.2 1.7 %copy.11 = f32[64,1024]{1,0:T(8,128)} copy(f32[64,1024]{1,0:T(8,128)} %detect.1) | data formatting | bytes 524288
